TPU v7x, 32 devices: a whole 2x2x4 slice. The times are simulated.
32 devices in a mesh: aux: 4 (over y, x), pair: 8 (over z, core).
Axes of the slice: x: 2, y: 2, z: 4, core: 2. Of those that a mesh axis runs over, the one named last changes fastest.
Arguments:
- df_tiles: bfloat16 [8, 128, 128, 128], P('pair', 'aux'), as said below
- pno_coeffs: bfloat16 [64, 3, 128, 64], P('pair'), may hold values from -0.5 to 0.5
- domains: int32 [64, 3], P('pair'), may hold values from 0 to 7, all different within a row; in each aligned block of 8 rows (0 to 7, 8 to 15, ...) at most 3 rows name the same one
- amplitudes: float32 [64, 64, 64], P('pair'), may hold values from -0.6 to 0.6
- exchange_ints: float32 [64, 64, 64], P('pair'), may hold values from -3 to 3
- pno_energy: float32 [64, 64], P('pair'), may hold values from 0.2 to 4
- pair_shift: float32 [64], P('pair'), may hold values from 0.3 to 1.5
- pno_count: int32 [64], P('pair'), may hold values from 16 to 64
Outputs:
- updated: float32 [64, 64, 64], P('pair')
Inputs may be any that keep to these rules, and one draw needn't show every extreme that they name: `domains`: among the pairs of one device no block is named by more than 3 pairs, and some block is named by exactly 3 of them. `df_tiles`: each tile is symmetric in its two PAO indices.
All inputs are finite; a program needn't handle non-finite values.
Results may differ from a plain program's by a relative error of at most 0.018.
Values may be sent and summed in bfloat16 or wider, within the bound.
A program may use at most 256 MiB of HBM per device.

v0:
```python
import math

import jax
import jax.numpy as jnp
from jax import lax
from jax.sharding import PartitionSpec as P


def apply_update(ladder, trial_amp, exch, energy_rows, energy_cols, shift, both):
    denom = energy_rows[:, :, None] + energy_cols[:, None, :] + shift[:, None, None]
    fresh = trial_amp - (exch + ladder) / denom
    return jnp.where(both, fresh, jnp.zeros_like(fresh))


def per_device(
    df_tiles, pno_coeffs, domains, amplitudes, exchange_ints, pno_energy, pair_shift, pno_count
):
    peers = lax.axis_size("pair")
    pair_count, domain_blocks, pao_width, pno_width = pno_coeffs.shape
    aux_local = df_tiles.shape[1]
    capacity = (pair_count * domain_blocks + peers - 1) // peers
    slot_count = peers * capacity
    request_count = pair_count * domain_blocks
    columns = jnp.arange(pno_width, dtype=jnp.int32)
    live = columns[None, :] < pno_count[:, None]
    masked = jnp.where(live[:, None, None, :], pno_coeffs, jnp.zeros_like(pno_coeffs))
    targets = domains.reshape(request_count)
    hits = (targets[:, None] == jnp.arange(peers, dtype=jnp.int32)[None, :]).astype(jnp.int32)
    before = jnp.cumsum(hits, axis=0) - hits
    ranks = jnp.sum(before * hits, axis=1)
    slots = targets * capacity + ranks
    select = (slots[:, None] == jnp.arange(slot_count, dtype=jnp.int32)[None, :]).astype(
        jnp.bfloat16
    )
    flat_coeffs = masked.reshape(request_count, pao_width * pno_width)
    outgoing = jnp.einsum(
        "rs,rk->sk", select, flat_coeffs, preferred_element_type=jnp.float32
    ).astype(jnp.bfloat16)
    outgoing = outgoing.reshape(peers, capacity, pao_width, pno_width)
    own_tile = df_tiles[0]
    arrived = lax.all_to_all(outgoing, "pair", split_axis=0, concat_axis=0, tiled=True)
    sources = arrived.shape[0]
    depth = arrived.shape[1]
    total = sources * depth
    group_size = math.gcd(total, 8)
    grouped = arrived.reshape(total // group_size, group_size, pao_width, pno_width)

    def project_group(group):
        half = jnp.einsum(
            "qmn,snp->sqmp", own_tile, group, preferred_element_type=jnp.float32
        ).astype(jnp.bfloat16)
        return jnp.einsum("smp,sqmr->sqpr", group, half, preferred_element_type=jnp.float32).astype(
            jnp.bfloat16
        )

    pieces = lax.map(project_group, grouped).reshape(
        sources, depth, aux_local, pno_width, pno_width
    )
    packed = pieces.reshape(sources, depth, aux_local * pno_width * pno_width)
    returned = lax.all_to_all(packed, "pair", split_axis=0, concat_axis=0, tiled=True)
    returned = returned.reshape(slot_count, returned.shape[2])
    owner_pair = jnp.arange(request_count, dtype=jnp.int32) // domain_blocks
    owner_sel = (owner_pair[:, None] == jnp.arange(pair_count, dtype=jnp.int32)[None, :]).astype(
        jnp.bfloat16
    )
    pair_sel = jnp.einsum(
        "rp,rs->ps", owner_sel, select, preferred_element_type=jnp.float32
    ).astype(jnp.bfloat16)
    sums = jnp.dot(pair_sel, returned, preferred_element_type=jnp.float32)
    full = sums.reshape(pair_count, aux_local, pno_width, pno_width)
    pair_ints = full.astype(jnp.bfloat16)
    both = live[:, :, None] & live[:, None, :]
    trial = jnp.where(both, amplitudes, jnp.zeros_like(amplitudes)).astype(jnp.bfloat16)
    inter = jnp.einsum(
        "pqac,pcd->pqad", pair_ints, trial, preferred_element_type=jnp.float32
    ).astype(jnp.bfloat16)
    partial_ladder = jnp.einsum(
        "pqad,pqbd->pab", inter, pair_ints, preferred_element_type=jnp.float32
    )
    ladder = lax.psum(partial_ladder.astype(jnp.bfloat16), "aux").astype(jnp.float32)
    return apply_update(ladder, amplitudes, exchange_ints, pno_energy, pno_energy, pair_shift, both)


def solution(mesh):
    placed = (
        P("pair", "aux", None, None),
        P("pair", None, None, None),
        P("pair", None),
        P("pair", None, None),
        P("pair", None, None),
        P("pair", None),
        P("pair"),
        P("pair"),
    )
    return jax.shard_map(
        per_device, mesh=mesh, in_specs=placed, out_specs=P("pair", None, None), check_vma=False
    )
```

profile of v0, /device:TPU:0, one launch (start us, length us, event | category | flops | bytes accessed | tf_op | source)
XLA Modules:
  0.0 380.0 jit_solution(4607345057817308631)
XLA Ops:
  6.5 0.0 copy-start
  6.5 0.8 copy.18
  7.4 0.1 reshape.93
  7.5 0.1 fusion.54
  7.6 0.2 select_reduce_fusion
  7.8 0.7 iota_compare_fusion.8
  8.5 1.1 broadcast_select_fusion
  9.7 0.4 copy.19
  10.0 0.6 reshape.94
  10.7 0.4 convolution_convert_fusion
  11.1 0.8 reshape.95
  11.9 1.0 copy.20
  13.0 6.3 %all-to-all-start = ((bf16[8,3,128,64]{2,3,1,0:T(8,128)(2,1)}), bf16[8,3,128,64]{2,3,1,0:T(8,128)(2,1)S(1)}, u32[]{:S(2)}, u32[]{:S(2)}) async-start(bf16[8,3,128,64]{2,3,1,0:T(8,128)(2,1)} %copy.20), calls=%async_computation | async-start | bytes 786432 | tf_op jit(solution)/shard_map/all_to_all | solution.py:41
  19.3 0.0 all-reduce.2.cloned.1.call-start
  19.3 12.5 %all-to-all-done = bf16[8,3,128,64]{2,3,1,0:T(8,128)(2,1)S(1)} async-done(((bf16[8,3,128,64]{2,3,1,0:T(8,128)(2,1)}), bf16[8,3,128,64]{2,3,1,0:T(8,128)(2,1)S(1)}, u32[]{:S(2)}, u32[]{:S(2)}) %all-to-all-start) | async-done | bytes 393248 | tf_op jit(solution)/shard_map/all_to_all | solution.py:41
  31.8 0.0 copy-done
  31.8 46.1 %while.10 = (s32[]{:T(128)}, bf16[3,8,32,64,64]{4,3,2,1,0:T(8,128)(2,1)}, bf16[3,8,128,64]{2,3,1,0:T(8,128)(2,1)S(1)}, bf16[32,128,128]{2,1,0:T(8,128)(2,1)S(1)}, s32[]{:T(128)}) while((s32[]{:T(128)}, bf16[3,8,32,64,64]{4,3,2,1,0:T(8,128)(2,1)}, bf16[3,8,128,64]{2,3,1,0:T(8,128)(2,1)S(1)}, bf16[32,128,128]{2,1,0:T(8,128)(2,1)S(1)}, ...), condition=%wide.region_3.4_spmd, body=%wide.region_2.3_spmd.sunk | while | flops 808452096 | bytes 15992381 | solution.py:56
  31.8 3.8 %convert_bitcast_fusion.2 = bf16[1,8,32,64,64]{3,4,2,1,0:T(8,128)(2,1)} fusion(bf16[32,128,128]{2,1,0:T(8,128)(2,1)S(1)} %get-tuple-element.80, bf16[3,8,128,64]{2,3,1,0:T(8,128)(2,1)S(1)} %get-tuple-element.79, s32[]{:T(128)} %get-tuple-element.72), kind=kOutput, calls=%fused_computation.2.clone.1 | convolution fusion | flops 808452096 | bytes 3408896 | tf_op jit(solution)/shard_map/while/body/eval_jaxpr/smp,sqmr->sqpr/dot_general | solution.py:52
  35.7 6.3 %copy.52 = bf16[1,8,32,64,64]{4,3,2,1,0:T(8,128)(2,1)} copy(bf16[1,8,32,64,64]{3,4,2,1,0:T(8,128)(2,1)} %convert_bitcast_fusion.2) | data formatting | bytes 4194304 | tf_op jit(solution)/shard_map/while/body/jit(dynamic_update_index_in_dim)/dynamic_update_slice | solution.py:56
  42.0 5.2 %constant_dynamic-update-slice_fusion.2 = bf16[3,8,32,64,64]{4,3,2,1,0:T(8,128)(2,1)} fusion(bf16[3,8,32,64,64]{4,3,2,1,0:T(8,128)(2,1)} %get-tuple-element.73, bf16[1,8,32,64,64]{4,3,2,1,0:T(8,128)(2,1)} %copy.52, s32[]{:T(128)} %get-tuple-element.72), kind=kLoop, calls=%fused_computation.8.clone.1 | loop fusion | bytes 8389120 | tf_op jit(solution)/shard_map/while/body/jit(dynamic_update_index_in_dim)/dynamic_update_slice | solution.py:56
  47.2 3.8 %convert_bitcast_fusion.2 = bf16[1,8,32,64,64]{3,4,2,1,0:T(8,128)(2,1)} fusion(bf16[32,128,128]{2,1,0:T(8,128)(2,1)S(1)} %get-tuple-element.80, bf16[3,8,128,64]{2,3,1,0:T(8,128)(2,1)S(1)} %get-tuple-element.79, s32[]{:T(128)} %get-tuple-element.72), kind=kOutput, calls=%fused_computation.2.clone.1 | convolution fusion | flops 808452096 | bytes 3408896 | tf_op jit(solution)/shard_map/while/body/eval_jaxpr/smp,sqmr->sqpr/dot_general | solution.py:52
  51.0 6.3 %copy.52 = bf16[1,8,32,64,64]{4,3,2,1,0:T(8,128)(2,1)} copy(bf16[1,8,32,64,64]{3,4,2,1,0:T(8,128)(2,1)} %convert_bitcast_fusion.2) | data formatting | bytes 4194304 | tf_op jit(solution)/shard_map/while/body/jit(dynamic_update_index_in_dim)/dynamic_update_slice | solution.py:56
  57.4 5.2 %constant_dynamic-update-slice_fusion.2 = bf16[3,8,32,64,64]{4,3,2,1,0:T(8,128)(2,1)} fusion(bf16[3,8,32,64,64]{4,3,2,1,0:T(8,128)(2,1)} %get-tuple-element.73, bf16[1,8,32,64,64]{4,3,2,1,0:T(8,128)(2,1)} %copy.52, s32[]{:T(128)} %get-tuple-element.72), kind=kLoop, calls=%fused_computation.8.clone.1 | loop fusion | bytes 8389120 | tf_op jit(solution)/shard_map/while/body/jit(dynamic_update_index_in_dim)/dynamic_update_slice | solution.py:56
  62.6 3.8 %convert_bitcast_fusion.2 = bf16[1,8,32,64,64]{3,4,2,1,0:T(8,128)(2,1)} fusion(bf16[32,128,128]{2,1,0:T(8,128)(2,1)S(1)} %get-tuple-element.80, bf16[3,8,128,64]{2,3,1,0:T(8,128)(2,1)S(1)} %get-tuple-element.79, s32[]{:T(128)} %get-tuple-element.72), kind=kOutput, calls=%fused_computation.2.clone.1 | convolution fusion | flops 808452096 | bytes 3408896 | tf_op jit(solution)/shard_map/while/body/eval_jaxpr/smp,sqmr->sqpr/dot_general | solution.py:52
  66.4 6.3 %copy.52 = bf16[1,8,32,64,64]{4,3,2,1,0:T(8,128)(2,1)} copy(bf16[1,8,32,64,64]{3,4,2,1,0:T(8,128)(2,1)} %convert_bitcast_fusion.2) | data formatting | bytes 4194304 | tf_op jit(solution)/shard_map/while/body/jit(dynamic_update_index_in_dim)/dynamic_update_slice | solution.py:56
  72.7 5.2 %constant_dynamic-update-slice_fusion.2 = bf16[3,8,32,64,64]{4,3,2,1,0:T(8,128)(2,1)} fusion(bf16[3,8,32,64,64]{4,3,2,1,0:T(8,128)(2,1)} %get-tuple-element.73, bf16[1,8,32,64,64]{4,3,2,1,0:T(8,128)(2,1)} %copy.52, s32[]{:T(128)} %get-tuple-element.72), kind=kLoop, calls=%fused_computation.8.clone.1 | loop fusion | bytes 8389120 | tf_op jit(solution)/shard_map/while/body/jit(dynamic_update_index_in_dim)/dynamic_update_slice | solution.py:56
  77.9 14.1 %reshape_reshape.3 = bf16[8,3,131072]{2,1,0:T(4,128)(2,1)} reshape(bf16[3,8,32,64,64]{4,3,2,1,0:T(8,128)(2,1)} %get-tuple-element.27) | data formatting | bytes 12582912 | tf_op jit(solution)/shard_map/reshape;reshape | solution.py:59
  92.0 189.8 %all_to_all.10 = bf16[8,3,131072]{2,1,0:T(4,128)(2,1)} all-to-all(bf16[8,3,131072]{2,1,0:T(4,128)(2,1)} %reshape_reshape.3), channel_id=1, replica_groups=mesh['aux'=4,'pair'=8] {'pair'}, dimensions={0} | all-to-all | bytes 12582912 | tf_op jit(solution)/shard_map/all_to_all | solution.py:60
  281.8 11.1 %reshape.97 = bf16[24,131072]{1,0:T(8,128)(2,1)} reshape(bf16[8,3,131072]{2,1,0:T(4,128)(2,1)} %all_to_all.10) | data formatting | bytes 12582912 | tf_op jit(solution)/shard_map/reshape | solution.py:61
  292.9 15.1 %dot_general.28 = bf16[32,64,64,24]{2,1,0,3:T(8,128)(2,1)} reshape(bf16[131072,24]{0,1:T(8,128)(2,1)} %bitcast.58) | data formatting | bytes 12582912 | tf_op jit(solution)/shard_map/dot_general | solution.py:69
  308.0 0.0 copy-start.1
  308.0 15.8 %fusion.22 = bf16[8,32,64,64]{3,0,2,1:T(8,128)(2,1)} fusion(bf16[32,64,64,24]{2,1,0,3:T(8,128)(2,1)} %dot_general.28, s32[24]{0:T(128)S(1)} %get-tuple-element.41, s32[24]{0:T(128)S(1)} %get-tuple-element.40), kind=kOutput, calls=%fused_computation.18 | convolution fusion | flops 51390400 | bytes 8388800 | tf_op jit(solution)/shard_map/dot_general | solution.py:69
  323.8 0.0 copy-done.1
  323.8 0.0 copy-start.2
  323.8 0.0 copy-start.3
  323.8 0.0 copy-start.4
  323.8 6.6 %fusion.36 = bf16[8,64,64]{2,1,0:T(8,128)(2,1)} fusion(bf16[8,32,64,64]{3,0,2,1:T(8,128)(2,1)} %fusion.22, f32[8,64,64]{2,1,0:T(8,128)S(1)} %copy-done.1, pred[8,64]{1,0:T(8,128)(4,1)S(1)} %iota_compare_fusion.8), kind=kOutput, calls=%fused_computation.20 | convolution fusion | flops 269582336 | bytes 2294272 | tf_op jit(solution)/shard_map/pqad,pqbd->pab/dot_general | solution.py:77
  330.3 0.0 all-reduce.2.cloned.1.call-update
  330.4 41.0 %all-reduce.2.cloned.1.call-done = bf16[8,64,64]{2,1,0:T(8,128)(2,1)} async-done(((bf16[8,64,64]{2,1,0:T(8,128)(2,1)}), bf16[8,64,64]{2,1,0:T(8,128)(2,1)}) %all-reduce.2.cloned.1.call-update) | async-done | bytes 65552 | tf_op jit(solution)/shard_map/psum | solution.py:80
  371.4 0.0 copy-done.2
  371.4 0.0 copy-done.3
  371.4 0.0 copy-done.4
  371.4 1.8 and_select_fusion
  (3 shorter events, 0.1 us)
Async XLA Ops:
  6.5 25.3 %copy-start = (bf16[1,32,128,128]{3,2,1,0:T(8,128)(2,1)S(1)}, bf16[1,32,128,128]{3,2,1,0:T(8,128)(2,1)}, u32[]{:S(2)}) copy-start(bf16[1,32,128,128]{3,2,1,0:T(8,128)(2,1)} %param.10) | copy-start | bytes 3145732
  13.0 18.9 %all-to-all-start = ((bf16[8,3,128,64]{2,3,1,0:T(8,128)(2,1)}), bf16[8,3,128,64]{2,3,1,0:T(8,128)(2,1)S(1)}, u32[]{:S(2)}, u32[]{:S(2)}) async-start(bf16[8,3,128,64]{2,3,1,0:T(8,128)(2,1)} %copy.20), calls=%async_computation | async-start | bytes 786432 | tf_op jit(solution)/shard_map/all_to_all | solution.py:41
  19.3 352.1 %all-reduce.2.cloned.1.call-start = ((), (), s32[]{:S(2)}) async-start(), calls=%async_computation.2 | async-start | bytes 262144 | tf_op jit(solution)/shard_map/psum | solution.py:80
  308.0 15.8 %copy-start.1 = (f32[8,64,64]{2,1,0:T(8,128)S(1)}, f32[8,64,64]{2,1,0:T(8,128)}, u32[]{:S(2)}) copy-start(f32[8,64,64]{2,1,0:T(8,128)} %param.13) | copy-start | bytes 393220
  323.8 47.6 %copy-start.2 = (f32[8,64,64]{2,1,0:T(8,128)S(1)}, f32[8,64,64]{2,1,0:T(8,128)}, u32[]{:S(2)}) copy-start(f32[8,64,64]{2,1,0:T(8,128)} %param.14) | copy-start | bytes 393220
  323.8 47.6 %copy-start.3 = (f32[8,64]{1,0:T(8,128)S(1)}, f32[8,64]{1,0:T(8,128)}, u32[]{:S(2)}) copy-start(f32[8,64]{1,0:T(8,128)} %param.15) | copy-start | bytes 6148
  323.8 47.6 %copy-start.4 = (f32[8]{0:T(128)S(1)}, f32[8]{0:T(128)}, u32[]{:S(2)}) copy-start(f32[8]{0:T(128)} %param.16) | copy-start | bytes 100
Sparse Core Ops, SparseCore 0:
  330.5 40.8 all-reduce.1
where the time goes:
time: 381 us; the launch traced here: 380 us
  blocking collectives  190 us (50%)
  local copies, waits for them, and re-layouts  78.6 us (21%)
  waiting for transfers between devices  53.5 us (14%)
  matrix products  34.2 us (9%)
  between operations  13.5 us (4%)
  starting transfers between devices  6.36 us (2%)
  other arithmetic  4 us (1%)
    all_to_all x1, blocking collectives, per_device(): lax.all_to_all(packed, 'pair', split_axis=0, concat_axis=0, tiled=True)  190 us
    psum x1, waiting for transfers between devices, per_device(): lax.psum(partial_ladder.astype(jnp.bfloat16), 'aux').astype(jnp.float32)  41 us
    dynamic_update_slice x6, local copies, waits for them, and re-layouts, per_device(): lax.map(project_group, grouped)  34.5 us
    dot_general x1, matrix products, per_device(): sums = jnp.dot(pair_sel, returned, preferred_element_type=jnp.float32)  15.8 us
    dot_general x1, local copies, waits for them, and re-layouts, per_device(): sums = jnp.dot(pair_sel, returned, preferred_element_type=jnp.float32)  15.1 us
    another operation x1, local copies, waits for them, and re-layouts, per_device(): packed = pieces.reshape(sources, depth, aux_local * pno_width * pno_width)  14.1 us
    all_to_all x1, waiting for transfers between devices, per_device(): lax.all_to_all(outgoing, 'pair', split_axis=0, concat_axis=0, tiled=True)  12.5 us
    dot_general x3, matrix products, project_group(): jnp.einsum('smp,sqmr->sqpr', group, half, preferred_element_type=jnp.floa...  11.5 us
  transfers between devices with their start and end apart: 2, of which 2 were waited for; matrix products, arithmetic and copies ran while one was open for 0% of the time, Pallas kernels for 0%

commit v1 on v0

--- a/solution.py
+++ b/solution.py
@@ -1,8 +1,11 @@
+import functools
 import math
 
 import jax
 import jax.numpy as jnp
 from jax import lax
+from jax.experimental import pallas as pl
+from jax.experimental.pallas import tpu as pltpu
 from jax.sharding import PartitionSpec as P
 
 
@@ -81,6 +84,264 @@
     return apply_update(ladder, amplitudes, exchange_ints, pno_energy, pno_energy, pair_shift, both)
 
 
+MESH = pl.DeviceIdType.MESH
+
+
+def ladder_kernel(packed_ref, coeff_ref, slot_ref, trial_ref, out_ref, tiles, halves, pieces,
+                  shares, send_sem, recv_sem, pass_send, pass_recv, twin_sem, aux_send, aux_recv,
+                  *, depth):
+    aux, pair = lax.axis_index("aux"), lax.axis_index("pair")
+    peers, groups = tiles.shape[0], shares.shape[0]
+    quarter = halves.shape[1] // (tiles.shape[3] // 2)
+    width = tiles.shape[3] // 2
+    pairs = trial_ref.shape[0]
+    domain = slot_ref.shape[0] // pairs
+    chip, core = pair // 2, pair % 2
+    twin = chip * 2 + 1 - core
+    chips = (chip + 1 - 2 * (chip % 2), 3 - chip, (chip + 2) % 4)
+
+    barrier = pltpu.get_barrier_semaphore()
+    for step in range(1, peers):
+        pl.semaphore_signal(barrier, inc=1, device_id={"pair": lax.rem(pair + step, peers)}, device_id_type=MESH)
+    for step in range(1, groups):
+        pl.semaphore_signal(barrier, inc=1, device_id={"aux": lax.rem(aux + step, groups)}, device_id_type=MESH)
+    pl.semaphore_wait(barrier, peers + groups - 2)
+
+    sends = []
+    for hop in range(3):
+        for side in range(2):
+            slot = hop * 2 + side
+            copy = pltpu.make_async_remote_copy(
+                src_ref=packed_ref.at[side],
+                dst_ref=tiles.at[pair, side],
+                send_sem=send_sem.at[slot],
+                recv_sem=recv_sem.at[hop * 2 + core],
+                device_id={"pair": chips[hop] * 2 + side},
+                device_id_type=MESH,
+            )
+            copy.start()
+            sends.append(copy)
+    whole = pltpu.make_async_remote_copy(
+        src_ref=packed_ref,
+        dst_ref=tiles.at[pair],
+        send_sem=twin_sem.at[0],
+        recv_sem=twin_sem.at[1],
+        device_id={"pair": twin},
+        device_id_type=MESH,
+    )
+    whole.start()
+
+    row = lax.broadcasted_iota(jnp.int32, (width, 2 * width), 0)
+    lane = lax.broadcasted_iota(jnp.int32, (width, 2 * width), 1)
+    upper = lane >= row
+    corner = lane == row + width
+    unroll = 4
+
+    def project(source, block, part):
+        coeffs = coeff_ref[block]
+
+        def some(group, carry):
+            for inner in range(unroll):
+                aux_fn = group * unroll + inner
+                first = pl.multiple_of(aux_fn * width, width)
+                folded = source(pl.ds(first, width)).astype(jnp.float32)
+                edge = source(pl.ds(pl.multiple_of(quarter * width + group * 16, 16), 16))
+                edge = edge[inner:inner + 1].astype(jnp.float32)
+                top = jnp.where(upper, folded, 0.0)
+                low = pltpu.roll(jnp.where(upper, 0.0, folded), width, 1)
+                low = jnp.where(corner, edge, low)
+                tri = jnp.concatenate([top, low], axis=0).astype(jnp.bfloat16)
+                half = jnp.dot(coeffs, tri, preferred_element_type=jnp.float32)
+                half += lax.dot_general(coeffs, tri, (((1,), (1,)), ((), ())), preferred_element_type=jnp.float32)
+                half = half.astype(jnp.bfloat16)
+                for rank in range(depth):
+                    halves[rank, pl.ds(first, width), :] = half[rank * width:(rank + 1) * width]
+            return carry
+
+        lax.fori_loop(0, quarter // unroll, some, 0)
+        span = quarter * width
+        for rank in range(depth):
+            piece = lax.dot_general(
+                coeffs[rank * width:(rank + 1) * width], halves[rank],
+                (((1,), (1,)), ((), ())), preferred_element_type=jnp.float32,
+            )
+            pieces[block * depth + rank, :, pl.ds(pl.multiple_of(part * span, span), span)] = piece.astype(jnp.bfloat16)
+
+    def own(part, carry):
+        project(lambda rows: packed_ref[part, rows, :], pair, part)
+        return carry
+
+    def arrived(block, part):
+        project(lambda rows: tiles[block, part, rows, :], block, part)
+
+    lax.fori_loop(0, 2, own, 0)
+    whole.wait_recv()
+
+    def from_twin(part, carry):
+        arrived(twin, part)
+        return carry
+
+    lax.fori_loop(0, 2, from_twin, 0)
+
+    passes = []
+    for hop in range(3):
+        handed = []
+        for side in range(2):
+            slot = hop * 2 + side
+            block = chips[hop] * 2 + side
+            pltpu.make_async_remote_copy(
+                src_ref=packed_ref.at[side], dst_ref=tiles.at[block, core],
+                send_sem=send_sem.at[slot], recv_sem=recv_sem.at[slot],
+                device_id={"pair": block}, device_id_type=MESH,
+            ).wait_recv()
+            copy = pltpu.make_async_remote_copy(
+                src_ref=tiles.at[block, core],
+                dst_ref=tiles.at[block, core],
+                send_sem=pass_send.at[slot],
+                recv_sem=pass_recv.at[slot],
+                device_id={"pair": twin},
+                device_id_type=MESH,
+            )
+            copy.start()
+            handed.append(copy)
+        passes += handed
+
+        def direct(side, carry, hop=hop):
+            arrived(chips[hop] * 2 + side, core)
+            return carry
+
+        lax.fori_loop(0, 2, direct, 0)
+        for side in range(2):
+            slot = hop * 2 + side
+            block = chips[hop] * 2 + side
+            pltpu.make_async_remote_copy(
+                src_ref=tiles.at[block, core], dst_ref=tiles.at[block, 1 - core],
+                send_sem=pass_send.at[slot], recv_sem=pass_recv.at[slot],
+                device_id={"pair": twin}, device_id_type=MESH,
+            ).wait_recv()
+
+        def passed(side, carry, hop=hop):
+            arrived(chips[hop] * 2 + side, 1 - core)
+            return carry
+
+        lax.fori_loop(0, 2, passed, 0)
+
+    def ladder_of(index):
+        total = pieces[slot_ref[index * domain]].astype(jnp.float32)
+        for step in range(1, domain):
+            total += pieces[slot_ref[index * domain + step]].astype(jnp.float32)
+        ints = total.astype(jnp.bfloat16)
+        trial = trial_ref[index]
+        span = trial.shape[0]
+        inter = jnp.concatenate(
+            [
+                jnp.dot(ints[:, at:at + span], trial, preferred_element_type=jnp.float32).astype(jnp.bfloat16)
+                for at in range(0, ints.shape[1], span)
+            ],
+            axis=1,
+        )
+        return lax.dot_general(inter, ints, (((1,), (1,)), ((), ())), preferred_element_type=jnp.float32)
+
+    def ladders(index, carry):
+        both = jnp.concatenate([ladder_of(index), ladder_of(index + pairs // 2)], axis=1)
+        shares[aux, pl.ds(pl.multiple_of(index * width, width), width), :] = both.astype(jnp.bfloat16)
+        return carry
+
+    lax.fori_loop(0, pairs // 2, ladders, 0)
+    exchange = []
+    for step in range(1, groups):
+        copy = pltpu.make_async_remote_copy(
+            src_ref=shares.at[aux],
+            dst_ref=shares.at[aux],
+            send_sem=aux_send.at[step - 1],
+            recv_sem=aux_recv.at[step - 1],
+            device_id={"aux": lax.rem(aux + step, groups)},
+            device_id_type=MESH,
+        )
+        copy.start()
+        exchange.append(copy)
+    for copy in sends + passes + [whole]:
+        copy.wait_send()
+    for step in range(1, groups):
+        sender = lax.rem(aux + groups - step, groups)
+        pltpu.make_async_remote_copy(
+            src_ref=shares.at[aux], dst_ref=shares.at[sender],
+            send_sem=aux_send.at[step - 1], recv_sem=aux_recv.at[step - 1],
+            device_id={"aux": sender}, device_id_type=MESH,
+        ).wait_recv()
+        exchange[step - 1].wait_send()
+    result = shares[0].astype(jnp.float32)
+    for step in range(1, groups):
+        result += shares[step].astype(jnp.float32)
+    out_ref[...] = result
+
+
+def fold_tiles(own_tile):
+    count, rows, _ = own_tile.shape
+    width = rows // 2
+    row = lax.broadcasted_iota(jnp.int32, (width, rows), 0)
+    lane = lax.broadcasted_iota(jnp.int32, (width, rows), 1)
+    top, bottom = own_tile[:, :width], own_tile[:, width:]
+    folded = jnp.where(lane >= row, top, jnp.roll(bottom, width, axis=2))
+    folded = jnp.where(lane == row, folded * jnp.bfloat16(0.5), folded)
+    edge = jnp.sum(jnp.where(lane == row + width, bottom.astype(jnp.float32) * 0.5, 0.0), axis=1)
+    edge = edge.astype(jnp.bfloat16).reshape(count // 4, 4, rows)
+    edge = jnp.pad(edge, ((0, 0), (0, 12), (0, 0))).reshape(2, -1, rows)
+    return jnp.concatenate([folded.reshape(2, -1, rows), edge], axis=1)
+
+
+def per_device_gathered(
+    df_tiles, pno_coeffs, domains, amplitudes, exchange_ints, pno_energy, pair_shift, pno_count
+):
+    peers, groups = lax.axis_size("pair"), lax.axis_size("aux")
+    pair_count, domain_blocks, pao_width, width = pno_coeffs.shape
+    request_count = pair_count * domain_blocks
+    depth = request_count // peers
+    columns = jnp.arange(width, dtype=jnp.int32)
+    live = columns[None, :] < pno_count[:, None]
+    masked = jnp.where(live[:, None, None, :], pno_coeffs, jnp.zeros_like(pno_coeffs))
+    targets = domains.reshape(request_count)
+    order = jnp.arange(request_count, dtype=jnp.int32)
+    earlier = (targets[:, None] == targets[None, :]) & (order[None, :] < order[:, None])
+    slots = targets * depth + jnp.sum(earlier.astype(jnp.int32), axis=1)
+    select = (slots[:, None] == order[None, :]).astype(jnp.bfloat16)
+    coeffs = jnp.einsum(
+        "rs,rnb->sbn", select, masked.reshape(request_count, pao_width, width),
+        preferred_element_type=jnp.float32,
+    ).astype(jnp.bfloat16)
+    coeffs = coeffs.reshape(peers, depth * width, pao_width)
+    both = live[:, :, None] & live[:, None, :]
+    trial = jnp.where(both, amplitudes, jnp.zeros_like(amplitudes)).astype(jnp.bfloat16)
+    twice = jnp.arange(2 * width, dtype=jnp.int32) // width
+    trial = jnp.where(twice[:, None] == twice[None, :], jnp.tile(trial, (1, 2, 2)), jnp.bfloat16(0))
+    packed = fold_tiles(df_tiles[0])
+    rows = packed.shape[1]
+    quarter = df_tiles.shape[1] // 2
+    vmem = pl.BlockSpec(memory_space=pltpu.VMEM)
+    dma = pltpu.SemaphoreType.DMA
+    ladder = pl.pallas_call(
+        functools.partial(ladder_kernel, depth=depth),
+        out_shape=jax.ShapeDtypeStruct((pair_count // 2 * width, 2 * width), jnp.float32),
+        in_specs=[vmem, vmem, pl.BlockSpec(memory_space=pltpu.SMEM), vmem],
+        out_specs=vmem,
+        scratch_shapes=[
+            pltpu.VMEM((peers, 2, rows, pao_width), jnp.bfloat16),
+            pltpu.VMEM((depth, quarter * width, pao_width), jnp.bfloat16),
+            pltpu.VMEM((request_count, width, 2 * quarter * width), jnp.bfloat16),
+            pltpu.VMEM((groups, pair_count // 2 * width, 2 * width), jnp.bfloat16),
+            dma((6,)), dma((6,)), dma((6,)), dma((6,)), dma((2,)),
+            dma((groups - 1,)), dma((groups - 1,)),
+        ],
+        compiler_params=pltpu.CompilerParams(
+            collective_id=0, has_side_effects=True, vmem_limit_bytes=48 * 1024 * 1024
+        ),
+        cost_estimate=pl.CostEstimate(flops=4000000000, bytes_accessed=4000000, transcendentals=0),
+    )(packed, coeffs, slots, trial)
+    ladder = ladder.reshape(pair_count // 2, width, 2, width).transpose(2, 0, 1, 3)
+    ladder = ladder.reshape(pair_count, width, width)
+    return apply_update(ladder, amplitudes, exchange_ints, pno_energy, pno_energy, pair_shift, both)
+
+
 def solution(mesh):
     placed = (
         P("pair", "aux", None, None),
@@ -92,6 +353,7 @@
         P("pair"),
         P("pair"),
     )
+    body = per_device_gathered if mesh.shape["pair"] == 8 else per_device
     return jax.shard_map(
-        per_device, mesh=mesh, in_specs=placed, out_specs=P("pair", None, None), check_vma=False
-    )
+        body, mesh=mesh, in_specs=placed, out_specs=P("pair", None, None), check_vma=False
+    )

time: 381 us -> 75.7 us (0.20)
  blocking collectives: 190 us -> 0 us
  local copies, waits for them, and re-layouts: 78.6 us -> 4.09 us
  Pallas kernels: 0 us -> 67.8 us
  waiting for transfers between devices: 53.5 us -> 0 us
  matrix products: 34.2 us -> 0.33 us
  between operations: 13.5 us -> 0.22 us
  starting transfers between devices: 6.36 us -> 0 us
    all_to_all x1 -> x0, blocking collectives: 190 us -> none  [per_device(): lax.all_to_all(packed, 'pair', split_axis=0, concat_axis=0, tiled=True)]
    pallas_call x0 -> x1, Pallas kernels: none -> 67.8 us  [per_device_gathered(): pl.pallas_call(functools.partial(ladder_kernel, depth=depth), out_shape=j...]
    psum x1 -> x0, waiting for transfers between devices: 41 us -> none  [per_device(): lax.psum(partial_ladder.astype(jnp.bfloat16), 'aux').astype(jnp.float32)]
    dynamic_update_slice x6 -> x0, local copies, waits for them, and re-layouts: 34.5 us -> none  [per_device(): lax.map(project_group, grouped)]
    dot_general x6 -> x1, matrix products: 34.2 us -> 0.33 us  [per_device_gathered(): jnp.einsum('rs,rnb->sbn', select, masked.reshape(request_count, pao_width...]
    dot_general x1 -> x0, local copies, waits for them, and re-layouts: 15.1 us -> none  [per_device(): sums = jnp.dot(pair_sel, returned, preferred_element_type=jnp.float32)]
    another operation x1 -> x2, local copies, waits for them, and re-layouts: 14.1 us -> 0.66 us  [per_device_gathered(): jnp.tile(trial, (1, 2, 2))]
    reshape x5 -> x2, local copies, waits for them, and re-layouts: 13.7 us -> 0.27 us  [the longest x1 0.19 us: per_device_gathered(): ladder.reshape(pair_count // 2, width, 2, width).transpose(2, 0, 1, 3)]
  transfers between devices with their start and end apart: 2 -> 0, of which waited for: 2 -> 0; matrix products, arithmetic and copies ran while one was open for 0% -> 0% of each run, Pallas kernels for 0% -> 0%
where the time goes in v1:
time: 75.7 us; the launch traced here: 74.8 us
  Pallas kernels  67.8 us (90%)
  local copies, waits for them, and re-layouts  4.09 us (5%)
  other arithmetic  2.31 us (3%)
    pallas_call x1, Pallas kernels, per_device_gathered(): pl.pallas_call(functools.partial(ladder_kernel, depth=depth), out_shape=j...  67.8 us
    slice x1, local copies, waits for them, and re-layouts, fold_tiles(): folded = jnp.where(lane >= row, top, jnp.roll(bottom, width, axis=2))  1.54 us
    unnamed x17, local copies, waits for them, and re-layouts  1.52 us

profile of v1, /device:TPU:0, one launch (start us, length us, event | category | flops | bytes accessed | tf_op | source)
XLA Modules:
  0.0 74.8 jit_solution(8996488796531647105)
XLA Ops:
  0.0 0.0 copy-start
  0.0 1.5 %fusion.9 = (bf16[32,64,64]{2,1,0:T(8,128)(2,1)S(1)}, bf16[32,64,64]{2,1,0:T(8,128)(2,1)S(1)}) fusion(bf16[32,128,128]{2,1,0:T(8,128)(2,1)} %bitcast.21), kind=kLoop, calls=%fused_computation.32 | loop fusion | bytes 1048576 | tf_op jit(solution)/shard_map/jit(_roll_static)/slice | solution.py:285
  1.6 0.0 copy-done
  1.6 0.4 multiply_select_fusion
  2.0 0.0 copy-start.5
  2.0 0.0 copy-start.7
  2.0 0.0 copy-start.2
  2.1 0.1 iota_compare_fusion
  2.1 0.2 select_reduce_fusion
  2.4 0.3 copy-done.5
  2.7 0.1 copy.17
  2.8 0.1 reshape.121
  2.9 0.2 convert_reduce_fusion
  3.1 0.0 copy-done.7
  3.1 0.1 iota_compare_fusion.5
  3.1 0.0 copy-done.2
  3.1 0.0 copy-start.1
  3.1 0.1 broadcast_select_fusion
  3.3 0.3 fusion
  3.6 0.1 copy.19
  3.7 0.4 copy-done.1
  4.1 0.1 fusion.2
  4.2 0.4 tile.4
  4.6 0.3 tile.10
  4.9 0.1 broadcast_compare_fusion
  5.0 0.0 copy-start.4
  5.1 0.0 copy-start.6
  5.1 67.8 %shard_map.82 = f32[256,128]{1,0:T(8,128)S(1)} custom-call(bf16[2,1088,128]{2,1,0:T(8,128)(2,1)S(1)} %pad_maximum_fusion.packed_ref, bf16[8,192,128]{2,1,0:T(8,128)(2,1)S(1)} %bitcast.20, s32[24]{0:T(128)S(1)} %multiply_add_fusion.slot_ref, bf16[8,128,128]{2,1,0:T(8,128)(2,1)S(1)} %broadcast_select_fusion.1.trial_ref), custom_call_target="tpu_custom_call" | custom-call | flops 4000000000 | bytes 4000000 | tf_op jit(solution)/shard_map/pallas_call | solution.py:322
  72.9 0.0 copy-start.3
  72.9 0.2 reshape.123
  73.1 0.0 copy-done.4
  73.1 0.0 copy-done.6
  73.2 0.7 copy-done.3
  73.9 0.9 %and_select_fusion = f32[8,64,64]{2,1,0:T(8,128)} fusion(f32[8,64,64]{2,1,0:T(8,128)S(1)} %copy-done.1, f32[8,64,64]{2,1,0:T(8,128)S(1)} %copy-done.3, f32[2,4,64,64]{3,2,1,0:T(8,128)S(1)} %copy.20, f32[8]{0:T(128)S(1)} %copy-done.6, f32[8,64]{1,0:T(8,128)S(1)} %copy-done.4, pred[8,64]{1,0:T(8,128)(4,1)S(1)} %iota_compare_fusion.5), kind=kLoop, calls=%fused_computation.8 | loop fusion | flops 229376 | bytes 526880 | tf_op jit(solution)/shard_map/jit(_where)/select_n | solution.py:15
  (8 shorter events, 0.1 us)
Async XLA Ops:
  0.0 1.6 %copy-start = (bf16[1,32,128,128]{3,2,1,0:T(8,128)(2,1)S(1)}, bf16[1,32,128,128]{3,2,1,0:T(8,128)(2,1)}, u32[]{:S(2)}) copy-start(bf16[1,32,128,128]{3,2,1,0:T(8,128)(2,1)} %param.8) | copy-start | bytes 3145732
  2.0 0.7 copy-start.5
  2.0 1.0 %copy-start.7 = (s32[8]{0:T(128)S(1)}, s32[8]{0:T(128)}, u32[]{:S(2)}) copy-start(s32[8]{0:T(128)} %param.15) | copy-start | bytes 100
  2.0 1.1 %copy-start.2 = (bf16[8,3,128,64]{2,3,1,0:T(8,128)(2,1)S(1)}, bf16[8,3,128,64]{2,3,1,0:T(8,128)(2,1)}, u32[]{:S(2)}) copy-start(bf16[8,3,128,64]{2,3,1,0:T(8,128)(2,1)} %param.9) | copy-start | bytes 1179652
  3.1 1.0 %copy-start.1 = (f32[8,64,64]{2,1,0:T(8,128)S(1)}, f32[8,64,64]{2,1,0:T(8,128)}, u32[]{:S(2)}) copy-start(f32[8,64,64]{2,1,0:T(8,128)} %param.11) | copy-start | bytes 393220
  5.0 68.1 %copy-start.4 = (f32[8,64]{1,0:T(8,128)S(1)}, f32[8,64]{1,0:T(8,128)}, u32[]{:S(2)}) copy-start(f32[8,64]{1,0:T(8,128)} %param.13) | copy-start | bytes 6148
  5.1 68.1 %copy-start.6 = (f32[8]{0:T(128)S(1)}, f32[8]{0:T(128)}, u32[]{:S(2)}) copy-start(f32[8]{0:T(128)} %param.14) | copy-start | bytes 100
  72.9 1.0 %copy-start.3 = (f32[8,64,64]{2,1,0:T(8,128)S(1)}, f32[8,64,64]{2,1,0:T(8,128)}, u32[]{:S(2)}) copy-start(f32[8,64,64]{2,1,0:T(8,128)} %param.12) | copy-start | bytes 393220

commit v2 on v1

--- a/solution.py
+++ b/solution.py
@@ -88,7 +88,8 @@
 
 
 def ladder_kernel(packed_ref, coeff_ref, slot_ref, trial_ref, out_ref, tiles, halves, pieces,
-                  shares, send_sem, recv_sem, pass_send, pass_recv, twin_sem, aux_send, aux_recv,
+                  shares, first_send, link_send, link_recv, pass_send, pass_recv, twin_sem, aux_send,
+                  aux_recv,
                   *, depth):
     aux, pair = lax.axis_index("aux"), lax.axis_index("pair")
     peers, groups = tiles.shape[0], shares.shape[0]
@@ -98,7 +99,7 @@
     domain = slot_ref.shape[0] // pairs
     chip, core = pair // 2, pair % 2
     twin = chip * 2 + 1 - core
-    chips = (chip + 1 - 2 * (chip % 2), 3 - chip, (chip + 2) % 4)
+    last = peers // 2 - 1
 
     barrier = pltpu.get_barrier_semaphore()
     for step in range(1, peers):
@@ -107,20 +108,57 @@
         pl.semaphore_signal(barrier, inc=1, device_id={"aux": lax.rem(aux + step, groups)}, device_id_type=MESH)
     pl.semaphore_wait(barrier, peers + groups - 2)
 
-    sends = []
-    for hop in range(3):
-        for side in range(2):
-            slot = hop * 2 + side
-            copy = pltpu.make_async_remote_copy(
-                src_ref=packed_ref.at[side],
-                dst_ref=tiles.at[pair, side],
-                send_sem=send_sem.at[slot],
-                recv_sem=recv_sem.at[hop * 2 + core],
-                device_id={"pair": chips[hop] * 2 + side},
-                device_id_type=MESH,
-            )
-            copy.start()
-            sends.append(copy)
+    def remote(source, target, send, recv, where):
+        return pltpu.make_async_remote_copy(
+            src_ref=source, dst_ref=target, send_sem=send, recv_sem=recv,
+            device_id={"pair": where}, device_id_type=MESH,
+        )
+
+    def onward(way):
+        return chip + 1 if way == 0 else chip - 1
+
+    def can_send(way):
+        return chip < last if way == 0 else chip > 0
+
+    def has_source(far, way):
+        return chip >= far if way == 0 else chip + far <= last
+
+    def block_of(far, way, side):
+        return (chip - far if way == 0 else chip + far) * 2 + side
+
+    def number(far, way, side):
+        return ((far - 1) * 2 + way) * 2 + side
+
+    def first(way, side):
+        return remote(packed_ref.at[side], tiles.at[pair, side], first_send.at[way * 2 + side],
+                      link_recv.at[number(1, way, core)], onward(way) * 2 + side)
+
+    def link(far, way, side):
+        block = block_of(far, way, side)
+        return remote(tiles.at[block, core], tiles.at[block, core], link_send.at[number(far, way, side)],
+                      link_recv.at[number(far + 1, way, side)], onward(way) * 2 + core)
+
+    def incoming(far, way, side):
+        block = block_of(far, way, side)
+        return remote(packed_ref.at[0], tiles.at[block, core], link_send.at[number(far, way, side)],
+                      link_recv.at[number(far, way, side)], twin)
+
+    def handed(far, way, side):
+        block = block_of(far, way, side)
+        return remote(tiles.at[block, core], tiles.at[block, core], pass_send.at[number(far, way, side)],
+                      pass_recv.at[number(far, way, side)], twin)
+
+    def handed_here(far, way, side):
+        block = block_of(far, way, side)
+        return remote(packed_ref.at[0], tiles.at[block, 1 - core], pass_send.at[number(far, way, side)],
+                      pass_recv.at[number(far, way, side)], twin)
+
+    for way in range(2):
+        @pl.when(can_send(way))
+        def _(way=way):
+            for side in range(2):
+                first(way, side).start()
+
     whole = pltpu.make_async_remote_copy(
         src_ref=packed_ref,
         dst_ref=tiles.at[pair],
@@ -183,48 +221,38 @@
 
     lax.fori_loop(0, 2, from_twin, 0)
 
-    passes = []
-    for hop in range(3):
-        handed = []
-        for side in range(2):
-            slot = hop * 2 + side
-            block = chips[hop] * 2 + side
-            pltpu.make_async_remote_copy(
-                src_ref=packed_ref.at[side], dst_ref=tiles.at[block, core],
-                send_sem=send_sem.at[slot], recv_sem=recv_sem.at[slot],
-                device_id={"pair": block}, device_id_type=MESH,
-            ).wait_recv()
-            copy = pltpu.make_async_remote_copy(
-                src_ref=tiles.at[block, core],
-                dst_ref=tiles.at[block, core],
-                send_sem=pass_send.at[slot],
-                recv_sem=pass_recv.at[slot],
-                device_id={"pair": twin},
-                device_id_type=MESH,
-            )
-            copy.start()
-            handed.append(copy)
-        passes += handed
-
-        def direct(side, carry, hop=hop):
-            arrived(chips[hop] * 2 + side, core)
-            return carry
-
-        lax.fori_loop(0, 2, direct, 0)
-        for side in range(2):
-            slot = hop * 2 + side
-            block = chips[hop] * 2 + side
-            pltpu.make_async_remote_copy(
-                src_ref=tiles.at[block, core], dst_ref=tiles.at[block, 1 - core],
-                send_sem=pass_send.at[slot], recv_sem=pass_recv.at[slot],
-                device_id={"pair": twin}, device_id_type=MESH,
-            ).wait_recv()
-
-        def passed(side, carry, hop=hop):
-            arrived(chips[hop] * 2 + side, 1 - core)
-            return carry
-
-        lax.fori_loop(0, 2, passed, 0)
+    for far in range(1, last + 1):
+        for way in range(2):
+            @pl.when(has_source(far, way))
+            def _(far=far, way=way):
+                for side in range(2):
+                    incoming(far, way, side).wait_recv()
+                    if far < last:
+                        @pl.when(can_send(way))
+                        def _(side=side):
+                            link(far, way, side).start()
+                    handed(far, way, side).start()
+
+        for way in range(2):
+            @pl.when(has_source(far, way))
+            def _(far=far, way=way):
+                def direct(side, carry):
+                    arrived(block_of(far, way, side), core)
+                    return carry
+
+                lax.fori_loop(0, 2, direct, 0)
+
+        for way in range(2):
+            @pl.when(has_source(far, way))
+            def _(far=far, way=way):
+                for side in range(2):
+                    handed_here(far, way, side).wait_recv()
+
+                def passed(side, carry):
+                    arrived(block_of(far, way, side), 1 - core)
+                    return carry
+
+                lax.fori_loop(0, 2, passed, 0)
 
     def ladder_of(index):
         total = pieces[slot_ref[index * domain]].astype(jnp.float32)
@@ -260,8 +288,22 @@
         )
         copy.start()
         exchange.append(copy)
-    for copy in sends + passes + [whole]:
-        copy.wait_send()
+    whole.wait_send()
+    for way in range(2):
+        @pl.when(can_send(way))
+        def _(way=way):
+            for side in range(2):
+                first(way, side).wait_send()
+
+        for far in range(1, last + 1):
+            @pl.when(has_source(far, way))
+            def _(far=far, way=way):
+                for side in range(2):
+                    handed(far, way, side).wait_send()
+                    if far < last:
+                        @pl.when(can_send(way))
+                        def _(side=side):
+                            link(far, way, side).wait_send()
     for step in range(1, groups):
         sender = lax.rem(aux + groups - step, groups)
         pltpu.make_async_remote_copy(
@@ -329,7 +371,7 @@
             pltpu.VMEM((depth, quarter * width, pao_width), jnp.bfloat16),
             pltpu.VMEM((request_count, width, 2 * quarter * width), jnp.bfloat16),
             pltpu.VMEM((groups, pair_count // 2 * width, 2 * width), jnp.bfloat16),
-            dma((6,)), dma((6,)), dma((6,)), dma((6,)), dma((2,)),
+            dma((4,)), dma((2 * peers,)), dma((2 * peers,)), dma((2 * peers,)), dma((2 * peers,)), dma((2,)),
             dma((groups - 1,)), dma((groups - 1,)),
         ],
         compiler_params=pltpu.CompilerParams(

time: 75.7 us -> 64.2 us (0.85)
  the two profiles are of different devices: /device:TPU:0 before, /device:TPU:1 now
where the time goes in v2:
time: 64.2 us; the launch traced here: 64 us
  Pallas kernels  57 us (89%)
  local copies, waits for them, and re-layouts  4.15 us (6%)
  other arithmetic  2.31 us (4%)
    pallas_call x1, Pallas kernels, per_device_gathered(): pl.pallas_call(functools.partial(ladder_kernel, depth=depth), out_shape=j...  57 us
    slice x1, local copies, waits for them, and re-layouts, fold_tiles(): folded = jnp.where(lane >= row, top, jnp.roll(bottom, width, axis=2))  1.59 us
    unnamed x17, local copies, waits for them, and re-layouts  1.52 us

profile of v2, /device:TPU:1, one launch (start us, length us, event | category | flops | bytes accessed | tf_op | source)
XLA Modules:
  0.0 64.0 jit_solution(7662440987563468187)
XLA Ops:
  0.0 0.0 copy-start
  0.0 1.6 %fusion.9 = (bf16[32,64,64]{2,1,0:T(8,128)(2,1)S(1)}, bf16[32,64,64]{2,1,0:T(8,128)(2,1)S(1)}) fusion(bf16[32,128,128]{2,1,0:T(8,128)(2,1)} %bitcast.21), kind=kLoop, calls=%fused_computation.32 | loop fusion | bytes 1048576 | tf_op jit(solution)/shard_map/jit(_roll_static)/slice | solution.py:327
  1.6 0.0 copy-done
  1.6 0.4 multiply_select_fusion
  2.1 0.0 copy-start.5
  2.1 0.0 copy-start.7
  2.1 0.0 copy-start.2
  2.1 0.1 iota_compare_fusion
  2.2 0.2 select_reduce_fusion
  2.4 0.3 copy-done.5
  2.8 0.1 copy.17
  2.8 0.1 reshape.121
  2.9 0.2 convert_reduce_fusion
  3.1 0.0 copy-done.7
  3.1 0.1 iota_compare_fusion.5
  3.2 0.0 copy-done.2
  3.2 0.0 copy-start.1
  3.2 0.1 broadcast_select_fusion
  3.3 0.3 fusion
  3.7 0.1 copy.19
  3.8 0.4 copy-done.1
  4.2 0.1 fusion.2
  4.3 0.4 tile.4
  4.7 0.3 tile.10
  5.0 0.1 broadcast_compare_fusion
  5.1 0.0 copy-start.4
  5.1 0.0 copy-start.6
  5.1 57.0 %shard_map.82 = f32[256,128]{1,0:T(8,128)S(1)} custom-call(bf16[2,1088,128]{2,1,0:T(8,128)(2,1)S(1)} %pad_maximum_fusion.packed_ref, bf16[8,192,128]{2,1,0:T(8,128)(2,1)S(1)} %bitcast.20, s32[24]{0:T(128)S(1)} %multiply_add_fusion.slot_ref, bf16[8,128,128]{2,1,0:T(8,128)(2,1)S(1)} %broadcast_select_fusion.1.trial_ref), custom_call_target="tpu_custom_call" | custom-call | flops 4000000000 | bytes 4000000 | tf_op jit(solution)/shard_map/pallas_call | solution.py:364
  62.2 0.0 copy-start.3
  62.2 0.2 reshape.123
  62.4 0.0 copy-done.4
  62.4 0.0 copy-done.6
  62.4 0.7 %copy-done.3 = f32[8,64,64]{2,1,0:T(8,128)S(1)} copy-done((f32[8,64,64]{2,1,0:T(8,128)S(1)}, f32[8,64,64]{2,1,0:T(8,128)}, u32[]{:S(2)}) %copy-start.3) | copy-done | bytes 131096
  63.1 0.9 %and_select_fusion = f32[8,64,64]{2,1,0:T(8,128)} fusion(f32[8,64,64]{2,1,0:T(8,128)S(1)} %copy-done.1, f32[8,64,64]{2,1,0:T(8,128)S(1)} %copy-done.3, f32[2,4,64,64]{3,2,1,0:T(8,128)S(1)} %copy.20, f32[8]{0:T(128)S(1)} %copy-done.6, f32[8,64]{1,0:T(8,128)S(1)} %copy-done.4, pred[8,64]{1,0:T(8,128)(4,1)S(1)} %iota_compare_fusion.5), kind=kLoop, calls=%fused_computation.8 | loop fusion | flops 229376 | bytes 526880 | tf_op jit(solution)/shard_map/jit(_where)/select_n | solution.py:15
  (8 shorter events, 0.1 us)
Async XLA Ops:
  0.0 1.6 %copy-start = (bf16[1,32,128,128]{3,2,1,0:T(8,128)(2,1)S(1)}, bf16[1,32,128,128]{3,2,1,0:T(8,128)(2,1)}, u32[]{:S(2)}) copy-start(bf16[1,32,128,128]{3,2,1,0:T(8,128)(2,1)} %param.8) | copy-start | bytes 3145732
  2.1 0.7 %copy-start.5 = (s32[8,3]{0,1:T(4,128)S(1)}, s32[8,3]{0,1:T(4,128)}, u32[]{:S(2)}) copy-start(s32[8,3]{0,1:T(4,128)} %param.10) | copy-start | bytes 292
  2.1 1.0 %copy-start.7 = (s32[8]{0:T(128)S(1)}, s32[8]{0:T(128)}, u32[]{:S(2)}) copy-start(s32[8]{0:T(128)} %param.15) | copy-start | bytes 100
  2.1 1.1 %copy-start.2 = (bf16[8,3,128,64]{2,3,1,0:T(8,128)(2,1)S(1)}, bf16[8,3,128,64]{2,3,1,0:T(8,128)(2,1)}, u32[]{:S(2)}) copy-start(bf16[8,3,128,64]{2,3,1,0:T(8,128)(2,1)} %param.9) | copy-start | bytes 1179652
  3.2 1.0 %copy-start.1 = (f32[8,64,64]{2,1,0:T(8,128)S(1)}, f32[8,64,64]{2,1,0:T(8,128)}, u32[]{:S(2)}) copy-start(f32[8,64,64]{2,1,0:T(8,128)} %param.11) | copy-start | bytes 393220
  5.1 57.3 %copy-start.4 = (f32[8,64]{1,0:T(8,128)S(1)}, f32[8,64]{1,0:T(8,128)}, u32[]{:S(2)}) copy-start(f32[8,64]{1,0:T(8,128)} %param.13) | copy-start | bytes 6148
  5.1 57.3 %copy-start.6 = (f32[8]{0:T(128)S(1)}, f32[8]{0:T(128)}, u32[]{:S(2)}) copy-start(f32[8]{0:T(128)} %param.14) | copy-start | bytes 100
  62.2 1.0 %copy-start.3 = (f32[8,64,64]{2,1,0:T(8,128)S(1)}, f32[8,64,64]{2,1,0:T(8,128)}, u32[]{:S(2)}) copy-start(f32[8,64,64]{2,1,0:T(8,128)} %param.12) | copy-start | bytes 393220

commit v3 on v2

--- a/solution.py
+++ b/solution.py
@@ -173,18 +173,19 @@
     lane = lax.broadcasted_iota(jnp.int32, (width, 2 * width), 1)
     upper = lane >= row
     corner = lane == row + width
-    unroll = 4
+    unroll = 8
 
     def project(source, block, part):
         coeffs = coeff_ref[block]
+        edges = source(pl.ds(quarter * width, quarter)).astype(jnp.float32)
+        edge_row = lax.broadcasted_iota(jnp.int32, edges.shape, 0)
 
         def some(group, carry):
             for inner in range(unroll):
                 aux_fn = group * unroll + inner
                 first = pl.multiple_of(aux_fn * width, width)
                 folded = source(pl.ds(first, width)).astype(jnp.float32)
-                edge = source(pl.ds(pl.multiple_of(quarter * width + group * 16, 16), 16))
-                edge = edge[inner:inner + 1].astype(jnp.float32)
+                edge = jnp.sum(jnp.where(edge_row == aux_fn, edges, 0.0), axis=0, keepdims=True)
                 top = jnp.where(upper, folded, 0.0)
                 low = pltpu.roll(jnp.where(upper, 0.0, folded), width, 1)
                 low = jnp.where(corner, edge, low)
@@ -221,16 +222,17 @@
 
     lax.fori_loop(0, 2, from_twin, 0)
 
-    for far in range(1, last + 1):
+    for far in range(1, last):
         for way in range(2):
             @pl.when(has_source(far, way))
             def _(far=far, way=way):
                 for side in range(2):
                     incoming(far, way, side).wait_recv()
-                    if far < last:
-                        @pl.when(can_send(way))
-                        def _(side=side):
-                            link(far, way, side).start()
+
+                    @pl.when(can_send(way))
+                    def _(side=side):
+                        link(far, way, side).start()
+
                     handed(far, way, side).start()
 
         for way in range(2):
@@ -253,6 +255,16 @@
                     return carry
 
                 lax.fori_loop(0, 2, passed, 0)
+
+    for way in range(2):
+        @pl.when(has_source(last, way))
+        def _(way=way):
+            for side in range(2):
+                incoming(last, way, side).wait_recv()
+                handed(last, way, side).start()
+                arrived(block_of(last, way, side), core)
+                handed_here(last, way, side).wait_recv()
+                arrived(block_of(last, way, side), 1 - core)
 
     def ladder_of(index):
         total = pieces[slot_ref[index * domain]].astype(jnp.float32)
@@ -327,8 +339,7 @@
     folded = jnp.where(lane >= row, top, jnp.roll(bottom, width, axis=2))
     folded = jnp.where(lane == row, folded * jnp.bfloat16(0.5), folded)
     edge = jnp.sum(jnp.where(lane == row + width, bottom.astype(jnp.float32) * 0.5, 0.0), axis=1)
-    edge = edge.astype(jnp.bfloat16).reshape(count // 4, 4, rows)
-    edge = jnp.pad(edge, ((0, 0), (0, 12), (0, 0))).reshape(2, -1, rows)
+    edge = edge.astype(jnp.bfloat16).reshape(2, count // 2, rows)
     return jnp.concatenate([folded.reshape(2, -1, rows), edge], axis=1)
 
 

time: 64.2 us -> 60.2 us (0.938)
  the two profiles are of different devices: /device:TPU:1 before, /device:TPU:0 now
where the time goes in v3:
time: 60.2 us; the launch traced here: 59.9 us
  Pallas kernels  53 us (88%)
  local copies, waits for them, and re-layouts  4.15 us (7%)
  other arithmetic  2.3 us (4%)
    pallas_call x1, Pallas kernels, per_device_gathered(): pl.pallas_call(functools.partial(ladder_kernel, depth=depth), out_shape=j...  53 us
    slice x1, local copies, waits for them, and re-layouts, fold_tiles(): folded = jnp.where(lane >= row, top, jnp.roll(bottom, width, axis=2))  1.59 us
    unnamed x17, local copies, waits for them, and re-layouts  1.54 us

profile of v3, /device:TPU:0, one launch (start us, length us, event | category | flops | bytes accessed | tf_op | source)
XLA Modules:
  0.0 59.9 jit_solution(3733879987617852390)
XLA Ops:
  0.0 0.0 copy-start
  0.0 1.6 %fusion.9 = (bf16[32,64,64]{2,1,0:T(8,128)(2,1)S(1)}, bf16[32,64,64]{2,1,0:T(8,128)(2,1)S(1)}) fusion(bf16[32,128,128]{2,1,0:T(8,128)(2,1)} %bitcast.20), kind=kLoop, calls=%fused_computation.32 | loop fusion | bytes 1048576 | tf_op jit(solution)/shard_map/jit(_roll_static)/slice | solution.py:339
  1.6 0.0 copy-done
  1.6 0.4 multiply_select_fusion
  2.1 0.0 copy-start.5
  2.1 0.0 copy-start.7
  2.1 0.0 copy-start.2
  2.1 0.1 iota_compare_fusion
  2.2 0.2 select_reduce_fusion
  2.4 0.3 copy-done.5
  2.8 0.1 copy.17
  2.8 0.1 reshape.117
  2.9 0.2 convert_reduce_fusion
  3.1 0.0 copy-done.7
  3.1 0.1 iota_compare_fusion.5
  3.2 0.0 copy-done.2
  3.2 0.0 copy-start.1
  3.2 0.1 broadcast_select_fusion
  3.3 0.3 fusion
  3.7 0.1 copy.19
  3.8 0.4 copy-done.1
  4.2 0.1 fusion.2
  4.3 0.4 tile.4
  4.7 0.2 tile.10
  5.0 0.1 broadcast_compare_fusion
  5.1 0.0 copy-start.4
  5.1 0.0 copy-start.6
  5.1 53.0 %shard_map.82 = f32[256,128]{1,0:T(8,128)S(1)} custom-call(bf16[2,1040,128]{2,1,0:T(8,128)(2,1)S(1)} %pad_maximum_fusion.packed_ref, bf16[8,192,128]{2,1,0:T(8,128)(2,1)S(1)} %bitcast.19, s32[24]{0:T(128)S(1)} %multiply_add_fusion.slot_ref, bf16[8,128,128]{2,1,0:T(8,128)(2,1)S(1)} %broadcast_select_fusion.1.trial_ref), custom_call_target="tpu_custom_call" | custom-call | flops 4000000000 | bytes 4000000 | tf_op jit(solution)/shard_map/pallas_call | solution.py:375
  58.1 0.0 copy-start.3
  58.1 0.2 reshape.119
  58.3 0.0 copy-done.4
  58.3 0.0 copy-done.6
  58.3 0.7 %copy-done.3 = f32[8,64,64]{2,1,0:T(8,128)S(1)} copy-done((f32[8,64,64]{2,1,0:T(8,128)S(1)}, f32[8,64,64]{2,1,0:T(8,128)}, u32[]{:S(2)}) %copy-start.3) | copy-done | bytes 131096
  59.0 0.9 %and_select_fusion = f32[8,64,64]{2,1,0:T(8,128)} fusion(f32[8,64,64]{2,1,0:T(8,128)S(1)} %copy-done.1, f32[8,64,64]{2,1,0:T(8,128)S(1)} %copy-done.3, f32[2,4,64,64]{3,2,1,0:T(8,128)S(1)} %copy.20, f32[8]{0:T(128)S(1)} %copy-done.6, f32[8,64]{1,0:T(8,128)S(1)} %copy-done.4, pred[8,64]{1,0:T(8,128)(4,1)S(1)} %iota_compare_fusion.5), kind=kLoop, calls=%fused_computation.8 | loop fusion | flops 229376 | bytes 526880 | tf_op jit(solution)/shard_map/jit(_where)/select_n | solution.py:15
  (7 shorter events, 0.1 us)
Async XLA Ops:
  0.0 1.6 %copy-start = (bf16[1,32,128,128]{3,2,1,0:T(8,128)(2,1)S(1)}, bf16[1,32,128,128]{3,2,1,0:T(8,128)(2,1)}, u32[]{:S(2)}) copy-start(bf16[1,32,128,128]{3,2,1,0:T(8,128)(2,1)} %param.8) | copy-start | bytes 3145732
  2.1 0.7 %copy-start.5 = (s32[8,3]{0,1:T(4,128)S(1)}, s32[8,3]{0,1:T(4,128)}, u32[]{:S(2)}) copy-start(s32[8,3]{0,1:T(4,128)} %param.10) | copy-start | bytes 292
  2.1 1.0 %copy-start.7 = (s32[8]{0:T(128)S(1)}, s32[8]{0:T(128)}, u32[]{:S(2)}) copy-start(s32[8]{0:T(128)} %param.15) | copy-start | bytes 100
  2.1 1.1 %copy-start.2 = (bf16[8,3,128,64]{2,3,1,0:T(8,128)(2,1)S(1)}, bf16[8,3,128,64]{2,3,1,0:T(8,128)(2,1)}, u32[]{:S(2)}) copy-start(bf16[8,3,128,64]{2,3,1,0:T(8,128)(2,1)} %param.9) | copy-start | bytes 1179652
  3.2 1.0 %copy-start.1 = (f32[8,64,64]{2,1,0:T(8,128)S(1)}, f32[8,64,64]{2,1,0:T(8,128)}, u32[]{:S(2)}) copy-start(f32[8,64,64]{2,1,0:T(8,128)} %param.11) | copy-start | bytes 393220
  5.1 53.2 %copy-start.4 = (f32[8,64]{1,0:T(8,128)S(1)}, f32[8,64]{1,0:T(8,128)}, u32[]{:S(2)}) copy-start(f32[8,64]{1,0:T(8,128)} %param.13) | copy-start | bytes 6148
  5.1 53.2 %copy-start.6 = (f32[8]{0:T(128)S(1)}, f32[8]{0:T(128)}, u32[]{:S(2)}) copy-start(f32[8]{0:T(128)} %param.14) | copy-start | bytes 100
  58.1 1.0 %copy-start.3 = (f32[8,64,64]{2,1,0:T(8,128)S(1)}, f32[8,64,64]{2,1,0:T(8,128)}, u32[]{:S(2)}) copy-start(f32[8,64,64]{2,1,0:T(8,128)} %param.12) | copy-start | bytes 393220

commit v4 on v3

--- a/solution.py
+++ b/solution.py
@@ -87,8 +87,8 @@
 MESH = pl.DeviceIdType.MESH
 
 
-def ladder_kernel(packed_ref, coeff_ref, slot_ref, trial_ref, out_ref, tiles, halves, pieces,
-                  shares, first_send, link_send, link_recv, pass_send, pass_recv, twin_sem, aux_send,
+def ladder_kernel(tile_ref, coeff_ref, slot_ref, trial_ref, out_ref, packed_ref, tiles, halves,
+                  pieces, shares, first_send, link_send, link_recv, pass_send, pass_recv, twin_sem, aux_send,
                   aux_recv,
                   *, depth):
     aux, pair = lax.axis_index("aux"), lax.axis_index("pair")
@@ -106,7 +106,6 @@
         pl.semaphore_signal(barrier, inc=1, device_id={"pair": lax.rem(pair + step, peers)}, device_id_type=MESH)
     for step in range(1, groups):
         pl.semaphore_signal(barrier, inc=1, device_id={"aux": lax.rem(aux + step, groups)}, device_id_type=MESH)
-    pl.semaphore_wait(barrier, peers + groups - 2)
 
     def remote(source, target, send, recv, where):
         return pltpu.make_async_remote_copy(
@@ -153,10 +152,35 @@
         return remote(packed_ref.at[0], tiles.at[block, 1 - core], pass_send.at[number(far, way, side)],
                       pass_recv.at[number(far, way, side)], twin)
 
-    for way in range(2):
-        @pl.when(can_send(way))
-        def _(way=way):
-            for side in range(2):
+    row = lax.broadcasted_iota(jnp.int32, (width, 2 * width), 0)
+    lane = lax.broadcasted_iota(jnp.int32, (width, 2 * width), 1)
+    upper = lane >= row
+    corner = lane == row + width
+    fold_row = lax.broadcasted_iota(jnp.int32, (quarter, 2 * width), 0)
+
+    def fold(part):
+        def some(group, edges):
+            for inner in range(4):
+                aux_fn = group * 4 + inner
+                top = tile_ref[part * quarter + aux_fn, :width].astype(jnp.float32)
+                bottom = tile_ref[part * quarter + aux_fn, width:].astype(jnp.float32)
+                folded = jnp.where(upper, top, pltpu.roll(bottom, width, 1))
+                folded = jnp.where(lane == row, folded * 0.5, folded)
+                packed_ref[part, pl.ds(pl.multiple_of(aux_fn * width, width), width), :] = folded.astype(jnp.bfloat16)
+                edge = jnp.sum(jnp.where(corner, bottom * 0.5, 0.0), axis=0, keepdims=True)
+                edges = jnp.where(fold_row == aux_fn, edge, edges)
+            return edges
+
+        edges = lax.fori_loop(0, quarter // 4, some, jnp.zeros((quarter, 2 * width), jnp.float32))
+        packed_ref[part, pl.ds(quarter * width, quarter), :] = edges.astype(jnp.bfloat16)
+
+    for side in range(2):
+        fold(side)
+        if side == 0:
+            pl.semaphore_wait(barrier, peers + groups - 2)
+        for way in range(2):
+            @pl.when(can_send(way))
+            def _(way=way, side=side):
                 first(way, side).start()
 
     whole = pltpu.make_async_remote_copy(
@@ -169,10 +193,6 @@
     )
     whole.start()
 
-    row = lax.broadcasted_iota(jnp.int32, (width, 2 * width), 0)
-    lane = lax.broadcasted_iota(jnp.int32, (width, 2 * width), 1)
-    upper = lane >= row
-    corner = lane == row + width
     unroll = 8
 
     def project(source, block, part):
@@ -287,7 +307,7 @@
         shares[aux, pl.ds(pl.multiple_of(index * width, width), width), :] = both.astype(jnp.bfloat16)
         return carry
 
-    lax.fori_loop(0, pairs // 2, ladders, 0)
+    lax.fori_loop(0, pairs // 2, ladders, 0, unroll=True)
     exchange = []
     for step in range(1, groups):
         copy = pltpu.make_async_remote_copy(
@@ -328,19 +348,6 @@
     for step in range(1, groups):
         result += shares[step].astype(jnp.float32)
     out_ref[...] = result
-
-
-def fold_tiles(own_tile):
-    count, rows, _ = own_tile.shape
-    width = rows // 2
-    row = lax.broadcasted_iota(jnp.int32, (width, rows), 0)
-    lane = lax.broadcasted_iota(jnp.int32, (width, rows), 1)
-    top, bottom = own_tile[:, :width], own_tile[:, width:]
-    folded = jnp.where(lane >= row, top, jnp.roll(bottom, width, axis=2))
-    folded = jnp.where(lane == row, folded * jnp.bfloat16(0.5), folded)
-    edge = jnp.sum(jnp.where(lane == row + width, bottom.astype(jnp.float32) * 0.5, 0.0), axis=1)
-    edge = edge.astype(jnp.bfloat16).reshape(2, count // 2, rows)
-    return jnp.concatenate([folded.reshape(2, -1, rows), edge], axis=1)
 
 
 def per_device_gathered(
@@ -365,11 +372,10 @@
     coeffs = coeffs.reshape(peers, depth * width, pao_width)
     both = live[:, :, None] & live[:, None, :]
     trial = jnp.where(both, amplitudes, jnp.zeros_like(amplitudes)).astype(jnp.bfloat16)
-    twice = jnp.arange(2 * width, dtype=jnp.int32) // width
-    trial = jnp.where(twice[:, None] == twice[None, :], jnp.tile(trial, (1, 2, 2)), jnp.bfloat16(0))
-    packed = fold_tiles(df_tiles[0])
-    rows = packed.shape[1]
+    before, after = (0, width), (width, 0)
+    trial = jnp.pad(trial, ((0, 0), before, before)) + jnp.pad(trial, ((0, 0), after, after))
     quarter = df_tiles.shape[1] // 2
+    rows = quarter * (width + 1)
     vmem = pl.BlockSpec(memory_space=pltpu.VMEM)
     dma = pltpu.SemaphoreType.DMA
     ladder = pl.pallas_call(
@@ -378,6 +384,7 @@
         in_specs=[vmem, vmem, pl.BlockSpec(memory_space=pltpu.SMEM), vmem],
         out_specs=vmem,
         scratch_shapes=[
+            pltpu.VMEM((2, rows, pao_width), jnp.bfloat16),
             pltpu.VMEM((peers, 2, rows, pao_width), jnp.bfloat16),
             pltpu.VMEM((depth, quarter * width, pao_width), jnp.bfloat16),
             pltpu.VMEM((request_count, width, 2 * quarter * width), jnp.bfloat16),
@@ -389,7 +396,7 @@
             collective_id=0, has_side_effects=True, vmem_limit_bytes=48 * 1024 * 1024
         ),
         cost_estimate=pl.CostEstimate(flops=4000000000, bytes_accessed=4000000, transcendentals=0),
-    )(packed, coeffs, slots, trial)
+    )(df_tiles[0], coeffs, slots, trial)
     ladder = ladder.reshape(pair_count // 2, width, 2, width).transpose(2, 0, 1, 3)
     ladder = ladder.reshape(pair_count, width, width)
     return apply_update(ladder, amplitudes, exchange_ints, pno_energy, pno_energy, pair_shift, both)

time: 60.2 us -> 58.9 us (0.978)
  Pallas kernels: 53 us -> 52.2 us
  local copies, waits for them, and re-layouts: 4.15 us -> 3.54 us
    unnamed x17 -> x13, local copies, waits for them, and re-layouts: 1.54 us -> 3.17 us
    slice x1 -> x0, local copies, waits for them, and re-layouts: 1.59 us -> none  [fold_tiles(): folded = jnp.where(lane >= row, top, jnp.roll(bottom, width, axis=2))]
    select_n x1, other arithmetic: 0.14 us -> 1.13 us  [per_device_gathered(): jnp.where(live[:, None, None, :], pno_coeffs, jnp.zeros_like(pno_coeffs))]
    pallas_call x1, Pallas kernels: 53 us -> 52.2 us  [per_device_gathered(): pl.pallas_call(functools.partial(ladder_kernel, depth=depth), out_shape=j...]
    another operation x2 -> x0, local copies, waits for them, and re-layouts: 0.65 us -> none  [per_device_gathered(): jnp.tile(trial, (1, 2, 2))]
where the time goes in v4:
time: 58.9 us; the launch traced here: 58.7 us
  Pallas kernels  52.2 us (89%)
  local copies, waits for them, and re-layouts  3.54 us (6%)
  other arithmetic  2.55 us (4%)
    pallas_call x1, Pallas kernels, per_device_gathered(): pl.pallas_call(functools.partial(ladder_kernel, depth=depth), out_shape=j...  52.2 us
    unnamed x13, local copies, waits for them, and re-layouts  3.17 us

profile of v4, /device:TPU:0, one launch (start us, length us, event | category | flops | bytes accessed | tf_op | source)
XLA Modules:
  0.0 58.7 jit_solution(17895419404231539648)
XLA Ops:
  0.0 0.8 %copy.17 = s32[8,3]{1,0:T(8,128)S(1)} copy(s32[8,3]{0,1:T(4,128)} %param.10) | data formatting | bytes 192 | tf_op args[2]
  0.8 0.1 reshape.80
  0.8 0.2 convert_reduce_fusion
  1.0 0.0 copy-start.5
  1.0 0.6 %copy-done.5 = s32[8]{0:T(128)S(1)} copy-done((s32[8]{0:T(128)S(1)}, s32[8]{0:T(128)}, u32[]{:S(2)}) %copy-start.5) | copy-done | bytes 56
  1.7 0.1 iota_compare_fusion.2
  1.8 1.1 %broadcast_select_fusion = bf16[8,3,128,64]{2,3,1,0:T(8,128)(2,1)S(1)} fusion(bf16[8,3,128,64]{2,3,1,0:T(8,128)(2,1)} %param.9, pred[8,64]{1,0:T(8,128)(4,1)S(1)} %iota_compare_fusion.2), kind=kLoop, calls=%fused_computation.3 | loop fusion | flops 196608 | bytes 786944 | tf_op jit(solution)/shard_map/jit(_where)/select_n | solution.py:362
  2.9 0.0 copy-start
  2.9 0.3 fusion
  3.2 0.0 copy-start.1
  3.3 0.1 copy.19
  3.3 0.9 %copy-done.1 = f32[8,64,64]{2,1,0:T(8,128)S(1)} copy-done((f32[8,64,64]{2,1,0:T(8,128)S(1)}, f32[8,64,64]{2,1,0:T(8,128)}, u32[]{:S(2)}) %copy-start.1) | copy-done | bytes 131096
  4.2 0.1 fusion.2
  4.3 0.1 pad_add_fusion.trial_ref
  4.4 0.0 copy-done
  4.5 52.2 %shard_map.82 = f32[256,128]{1,0:T(8,128)S(1)} custom-call(bf16[32,128,128]{2,1,0:T(8,128)(2,1)S(1)} %bitcast.19, bf16[8,192,128]{2,1,0:T(8,128)(2,1)S(1)} %bitcast.18, s32[24]{0:T(128)S(1)} %multiply_add_fusion.slot_ref, bf16[8,128,128]{2,1,0:T(8,128)(2,1)S(1)} %pad_add_fusion.trial_ref), custom_call_target="tpu_custom_call" | custom-call | flops 4000000000 | bytes 4000000 | tf_op jit(solution)/shard_map/pallas_call | solution.py:381
  56.6 0.2 reshape.82
  56.8 0.0 copy-start.2
  56.8 0.0 copy-start.3
  56.8 0.0 copy-start.4
  56.9 0.9 %copy-done.2 = f32[8,64,64]{2,1,0:T(8,128)S(1)} copy-done((f32[8,64,64]{2,1,0:T(8,128)S(1)}, f32[8,64,64]{2,1,0:T(8,128)}, u32[]{:S(2)}) %copy-start.2) | copy-done | bytes 131096
  57.8 0.0 copy-done.3
  57.8 0.0 copy-done.4
  57.8 0.9 %and_select_fusion = f32[8,64,64]{2,1,0:T(8,128)} fusion(f32[8,64,64]{2,1,0:T(8,128)S(1)} %copy-done.1, f32[8,64,64]{2,1,0:T(8,128)S(1)} %copy-done.2, f32[4,64,2,64]{3,1,0,2:T(8,128)S(1)} %copy.20, f32[8]{0:T(128)S(1)} %copy-done.4, f32[8,64]{1,0:T(8,128)S(1)} %copy-done.3, pred[8,64]{1,0:T(8,128)(4,1)S(1)} %iota_compare_fusion.2), kind=kLoop, calls=%fused_computation.4 | loop fusion | flops 229376 | bytes 526880 | tf_op jit(solution)/shard_map/jit(_where)/select_n | solution.py:15
  (2 shorter events, 0.0 us)
Async XLA Ops:
  1.0 0.7 %copy-start.5 = (s32[8]{0:T(128)S(1)}, s32[8]{0:T(128)}, u32[]{:S(2)}) copy-start(s32[8]{0:T(128)} %param.15) | copy-start | bytes 100
  2.9 1.6 %copy-start = (bf16[1,32,128,128]{3,2,1,0:T(8,128)(2,1)S(1)}, bf16[1,32,128,128]{3,2,1,0:T(8,128)(2,1)}, u32[]{:S(2)}) copy-start(bf16[1,32,128,128]{3,2,1,0:T(8,128)(2,1)} %param.8) | copy-start | bytes 3145732
  3.2 1.0 %copy-start.1 = (f32[8,64,64]{2,1,0:T(8,128)S(1)}, f32[8,64,64]{2,1,0:T(8,128)}, u32[]{:S(2)}) copy-start(f32[8,64,64]{2,1,0:T(8,128)} %param.11) | copy-start | bytes 393220
  56.8 1.0 %copy-start.2 = (f32[8,64,64]{2,1,0:T(8,128)S(1)}, f32[8,64,64]{2,1,0:T(8,128)}, u32[]{:S(2)}) copy-start(f32[8,64,64]{2,1,0:T(8,128)} %param.12) | copy-start | bytes 393220
  56.8 0.9 %copy-start.3 = (f32[8,64]{1,0:T(8,128)S(1)}, f32[8,64]{1,0:T(8,128)}, u32[]{:S(2)}) copy-start(f32[8,64]{1,0:T(8,128)} %param.13) | copy-start | bytes 6148
  56.8 0.9 %copy-start.4 = (f32[8]{0:T(128)S(1)}, f32[8]{0:T(128)}, u32[]{:S(2)}) copy-start(f32[8]{0:T(128)} %param.14) | copy-start | bytes 100

commit v5 on v4

--- a/solution.py
+++ b/solution.py
@@ -193,7 +193,7 @@
     )
     whole.start()
 
-    unroll = 8
+    unroll = 16
 
     def project(source, block, part):
         coeffs = coeff_ref[block]

time: 58.9 us -> 58.2 us (0.988)
  Pallas kernels: 52.2 us -> 51.5 us
    pallas_call x1, Pallas kernels: 52.2 us -> 51.5 us  [per_device_gathered(): pl.pallas_call(functools.partial(ladder_kernel, depth=depth), out_shape=j...]
where the time goes in v5:
time: 58.2 us; the launch traced here: 58 us
  Pallas kernels  51.5 us (88%)
  local copies, waits for them, and re-layouts  3.54 us (6%)
  other arithmetic  2.55 us (4%)
    pallas_call x1, Pallas kernels, per_device_gathered(): pl.pallas_call(functools.partial(ladder_kernel, depth=depth), out_shape=j...  51.5 us
    unnamed x13, local copies, waits for them, and re-layouts  3.17 us

profile of v5, /device:TPU:0, one launch (start us, length us, event | category | flops | bytes accessed | tf_op | source)
XLA Modules:
  0.0 58.0 jit_solution(14734260085056201638)
XLA Ops:
  0.0 0.8 %copy.17 = s32[8,3]{1,0:T(8,128)S(1)} copy(s32[8,3]{0,1:T(4,128)} %param.10) | data formatting | bytes 192 | tf_op args[2]
  0.8 0.1 reshape.80
  0.8 0.2 convert_reduce_fusion
  1.0 0.0 copy-start.5
  1.0 0.6 %copy-done.5 = s32[8]{0:T(128)S(1)} copy-done((s32[8]{0:T(128)S(1)}, s32[8]{0:T(128)}, u32[]{:S(2)}) %copy-start.5) | copy-done | bytes 56
  1.7 0.1 iota_compare_fusion.2
  1.8 1.1 %broadcast_select_fusion = bf16[8,3,128,64]{2,3,1,0:T(8,128)(2,1)S(1)} fusion(bf16[8,3,128,64]{2,3,1,0:T(8,128)(2,1)} %param.9, pred[8,64]{1,0:T(8,128)(4,1)S(1)} %iota_compare_fusion.2), kind=kLoop, calls=%fused_computation.3 | loop fusion | flops 196608 | bytes 786944 | tf_op jit(solution)/shard_map/jit(_where)/select_n | solution.py:362
  2.9 0.0 copy-start
  2.9 0.3 fusion
  3.2 0.0 copy-start.1
  3.3 0.1 copy.19
  3.3 0.9 %copy-done.1 = f32[8,64,64]{2,1,0:T(8,128)S(1)} copy-done((f32[8,64,64]{2,1,0:T(8,128)S(1)}, f32[8,64,64]{2,1,0:T(8,128)}, u32[]{:S(2)}) %copy-start.1) | copy-done | bytes 131096
  4.2 0.1 fusion.2
  4.3 0.1 pad_add_fusion.trial_ref
  4.4 0.0 copy-done
  4.5 51.5 %shard_map.82 = f32[256,128]{1,0:T(8,128)S(1)} custom-call(bf16[32,128,128]{2,1,0:T(8,128)(2,1)S(1)} %bitcast.19, bf16[8,192,128]{2,1,0:T(8,128)(2,1)S(1)} %bitcast.18, s32[24]{0:T(128)S(1)} %multiply_add_fusion.slot_ref, bf16[8,128,128]{2,1,0:T(8,128)(2,1)S(1)} %pad_add_fusion.trial_ref), custom_call_target="tpu_custom_call" | custom-call | flops 4000000000 | bytes 4000000 | tf_op jit(solution)/shard_map/pallas_call | solution.py:381
  55.9 0.2 reshape.82
  56.1 0.0 copy-start.2
  56.1 0.0 copy-start.3
  56.2 0.0 copy-start.4
  56.2 0.9 %copy-done.2 = f32[8,64,64]{2,1,0:T(8,128)S(1)} copy-done((f32[8,64,64]{2,1,0:T(8,128)S(1)}, f32[8,64,64]{2,1,0:T(8,128)}, u32[]{:S(2)}) %copy-start.2) | copy-done | bytes 131096
  57.1 0.0 copy-done.3
  57.1 0.0 copy-done.4
  57.1 0.9 %and_select_fusion = f32[8,64,64]{2,1,0:T(8,128)} fusion(f32[8,64,64]{2,1,0:T(8,128)S(1)} %copy-done.1, f32[8,64,64]{2,1,0:T(8,128)S(1)} %copy-done.2, f32[4,64,2,64]{3,1,0,2:T(8,128)S(1)} %copy.20, f32[8]{0:T(128)S(1)} %copy-done.4, f32[8,64]{1,0:T(8,128)S(1)} %copy-done.3, pred[8,64]{1,0:T(8,128)(4,1)S(1)} %iota_compare_fusion.2), kind=kLoop, calls=%fused_computation.4 | loop fusion | flops 229376 | bytes 526880 | tf_op jit(solution)/shard_map/jit(_where)/select_n | solution.py:15
  (2 shorter events, 0.0 us)
Async XLA Ops:
  1.0 0.7 %copy-start.5 = (s32[8]{0:T(128)S(1)}, s32[8]{0:T(128)}, u32[]{:S(2)}) copy-start(s32[8]{0:T(128)} %param.15) | copy-start | bytes 100
  2.9 1.6 %copy-start = (bf16[1,32,128,128]{3,2,1,0:T(8,128)(2,1)S(1)}, bf16[1,32,128,128]{3,2,1,0:T(8,128)(2,1)}, u32[]{:S(2)}) copy-start(bf16[1,32,128,128]{3,2,1,0:T(8,128)(2,1)} %param.8) | copy-start | bytes 3145732
  3.2 1.0 %copy-start.1 = (f32[8,64,64]{2,1,0:T(8,128)S(1)}, f32[8,64,64]{2,1,0:T(8,128)}, u32[]{:S(2)}) copy-start(f32[8,64,64]{2,1,0:T(8,128)} %param.11) | copy-start | bytes 393220
  56.1 1.0 %copy-start.2 = (f32[8,64,64]{2,1,0:T(8,128)S(1)}, f32[8,64,64]{2,1,0:T(8,128)}, u32[]{:S(2)}) copy-start(f32[8,64,64]{2,1,0:T(8,128)} %param.12) | copy-start | bytes 393220
  56.1 0.9 %copy-start.3 = (f32[8,64]{1,0:T(8,128)S(1)}, f32[8,64]{1,0:T(8,128)}, u32[]{:S(2)}) copy-start(f32[8,64]{1,0:T(8,128)} %param.13) | copy-start | bytes 6148
  56.2 0.9 %copy-start.4 = (f32[8]{0:T(128)S(1)}, f32[8]{0:T(128)}, u32[]{:S(2)}) copy-start(f32[8]{0:T(128)} %param.14) | copy-start | bytes 100
